TPU v7x, 32 devices: a whole 2x2x4 slice. The times are simulated.
32 devices in a mesh: grp: 2 (over y), row: 4 (over x, core), col: 4 (over z).
Axes of the slice: x: 2, y: 2, z: 4, core: 2. Of those that a mesh axis runs over, the one named last changes fastest.
Arguments:
- video: bfloat16 [514, 32, 512], P('grp', 'row', 'col'), parts along dimension 0, may hold values from -6 to 6, as said below
- filters: float32 [4, 2, 7, 7], replicated, may hold values from -0.875 to 0.875
- start_basis: float32 [256, 64], replicated, may hold values from -6 to 6
Outputs:
- basis: float32 [512, 64], P('grp'), parts along dimension 0
- modes: float32 [16, 128, 256], P(('grp', 'row'), 'col'), parts along dimension 0
There are 2 independent parts, one for each index of `grp`. A program takes and returns all parts, laid end to end along the dimension named above; an argument that names none is the same for every part. Nothing has to cross between parts.
Inputs may be any that keep to these rules, and one draw needn't show every extreme that they name: `video`: grey levels: a fixed texture plus a per-pixel oscillation in time.
All inputs are finite; a program needn't handle non-finite values.
Results may differ from a plain program's by a relative error of at most 0.0034.
Values may be sent and summed in bfloat16 or wider, within the bound.
No kernel may reach another device: no remote copies, remote signals or barrier semaphores. Data moves between devices by JAX's collectives and lax.ppermute only.
A program may use at most 64 MiB of HBM per device.

v0:
```python
import jax
import jax.numpy as jnp
from jax import lax
from jax.sharding import PartitionSpec as P

FRAMES = 256
MODES = 64
ORIENT = 4
TAPS = 7
SWEEPS = 2


def padded_2(array, sides, width):
    for axis, dim in sides:
        size, length = (lax.axis_size(axis), array.shape[dim])
        up = [(i, (i + 1) % size) for i in range(size - 1)]
        down = [(j, i) for i, j in up]
        last = lax.slice_in_dim(array, length - width, length, axis=dim)
        first = lax.slice_in_dim(array, 0, width, axis=dim)
        before = lax.ppermute(last, axis, up)
        after = lax.ppermute(first, axis, down)
        array = jnp.concatenate([before, array, after], axis=dim)
    return array


def orthonormal(stacked):
    inner = jnp.dot(stacked.T, stacked, precision=lax.Precision.HIGHEST)
    factor = jnp.linalg.cholesky(inner)
    return lax.linalg.triangular_solve(
        factor, stacked, left_side=False, lower=True, transpose_a=True
    )


def on_device(video, filters, start_basis):
    tile_rows = video.shape[1]
    tile_cols = video.shape[2]
    padded = padded_2(video, (("row", 1), ("col", 2)), 3)

    def orient(taps):
        kernels = taps.reshape(2, 1, TAPS, TAPS)
        lifted = padded.astype(jnp.float32)[:, None]
        response = lax.conv_general_dilated(
            lifted, kernels, (1, 1), "VALID", precision=lax.Precision.HIGHEST
        )
        real_part = response[:, 0]
        imag_part = response[:, 1]
        prod_real = real_part[1:] * real_part[:-1] + imag_part[1:] * imag_part[:-1]
        prod_imag = imag_part[1:] * real_part[:-1] - real_part[1:] * imag_part[:-1]
        motion = prod_imag / jnp.sqrt(prod_real * prod_real + prod_imag * prod_imag + 1.0)
        pooled = motion.reshape(FRAMES, tile_rows // 4, 4, tile_cols // 4, 4).mean(axis=(2, 4))
        return pooled.astype(jnp.bfloat16)

    stacked = lax.map(orient, filters)
    flat = jnp.transpose(stacked, (1, 0, 2, 3)).reshape(FRAMES, -1)
    devices_all = lax.axis_size("row") * lax.axis_size("col")
    npix_all = flat.shape[1] * devices_all
    basis_now = start_basis
    local_gram = jnp.dot(flat, flat.T, preferred_element_type=jnp.float32)
    gram = lax.psum(local_gram, ("row", "col")) / npix_all
    for sweep in range(SWEEPS):
        basis_now = orthonormal(jnp.dot(gram, basis_now, precision=lax.Precision.HIGHEST))
    projected = jnp.dot(basis_now.astype(jnp.bfloat16).T, flat, preferred_element_type=jnp.float32)
    fields = projected.reshape(MODES, ORIENT, tile_rows // 4, tile_cols // 4)
    modes = jnp.transpose(fields, (2, 3, 1, 0)).reshape(
        tile_rows // 4, tile_cols // 4, ORIENT * MODES
    )
    return (basis_now, modes)


def solution(mesh):
    return jax.shard_map(
        on_device,
        mesh=mesh,
        in_specs=(P("grp", "row", "col"), P(), P()),
        out_specs=(P("grp", None), P(("grp", "row"), "col", None)),
        check_vma=False,
    )
```

profile of v0, /device:TPU:1, one launch (start us, length us, event | category | flops | bytes accessed | tf_op | source)
XLA Modules:
  0.0 571.4 jit_solution(12141925055525839283)
XLA Ops:
  7.2 0.0 copy-start
  7.2 0.0 all-reduce.2.cloned.1.call-start
  7.2 1.5 copy.25
  8.7 0.1 fusion.24
  8.8 4.5 collective-permute-start
  13.3 1.9 collective-permute-start.1
  15.2 1.7 collective-permute-done
  16.9 4.4 collective-permute-done.1
  21.4 3.2 collective-permute-start.2
  24.6 1.3 collective-permute-start.3
  25.9 3.4 collective-permute-done.3
  29.3 1.8 pad_maximum_fusion
  31.1 414.1 %while.10 = (s32[]{:T(128)}, bf16[4,256,2,32]{1,3,2,0:T(8,128)(2,1)S(1)}, bf16[257,14,134]{0,2,1:T(8,128)(2,1)}, f32[4,2,7,7]{3,1,2,0:T(2,128)}, s32[]{:T(128)}) while((s32[]{:T(128)}, bf16[4,256,2,32]{1,3,2,0:T(8,128)(2,1)S(1)}, bf16[257,14,134]{0,2,1:T(8,128)(2,1)}, f32[4,2,7,7]{3,1,2,0:T(2,128)}, s32[]{:T(128)}) %tuple.29), condition=%wide.region_2.3_spmd, body=%wide.region_0.2_spmd.sunk | while | flops 312647680 | bytes 15818389 | solution.py:53
  31.1 0.7 dynamic-slice_bitcast_fusion.2
  31.8 0.2 copy.40
  32.0 87.6 %fusion.42 = f32[257,2,8,128]{0,1,3,2:T(2,128)S(1)} fusion(f32[2,1,7,7]{1,0,3,2:T(2,128)S(1)} %copy.40, bf16[257,1,14,134]{0,3,2,1:T(8,128)(2,1)} %bitcast.71), kind=kOutput, calls=%fused_computation.clone.1 | convolution fusion | flops 309485568 | bytes 3070000 | tf_op jit(solution)/shard_map/while/body/eval_jaxpr/conv_general_dilated | solution.py:42
  119.6 13.7 %multiply_reduce_fusion.4 = (f32[256,8,128]{0,2,1:T(8,128)S(1)}, f32[256,8,128]{0,2,1:T(8,128)S(1)}) fusion(f32[257,2,8,128]{0,1,3,2:T(2,128)S(1)} %fusion.42), kind=kLoop, calls=%fused_computation.3.clone.1 | loop fusion | flops 1835008 | bytes 6291456 | tf_op jit(solution)/shard_map/while/body/eval_jaxpr/mul | solution.py:49
  133.3 0.3 mul.70
  133.6 0.3 sub.13
  134.0 0.6 multiply_reduce_fusion.5
  134.6 0.7 dynamic-slice_bitcast_fusion.2
  135.3 0.2 copy.40
  135.5 87.6 %fusion.42 = f32[257,2,8,128]{0,1,3,2:T(2,128)S(1)} fusion(f32[2,1,7,7]{1,0,3,2:T(2,128)S(1)} %copy.40, bf16[257,1,14,134]{0,3,2,1:T(8,128)(2,1)} %bitcast.71), kind=kOutput, calls=%fused_computation.clone.1 | convolution fusion | flops 309485568 | bytes 3070000 | tf_op jit(solution)/shard_map/while/body/eval_jaxpr/conv_general_dilated | solution.py:42
  223.1 13.7 %multiply_reduce_fusion.4 = (f32[256,8,128]{0,2,1:T(8,128)S(1)}, f32[256,8,128]{0,2,1:T(8,128)S(1)}) fusion(f32[257,2,8,128]{0,1,3,2:T(2,128)S(1)} %fusion.42), kind=kLoop, calls=%fused_computation.3.clone.1 | loop fusion | flops 1835008 | bytes 6291456 | tf_op jit(solution)/shard_map/while/body/eval_jaxpr/mul | solution.py:49
  236.8 0.3 mul.70
  237.1 0.3 sub.13
  237.4 0.6 multiply_reduce_fusion.5
  238.1 0.7 dynamic-slice_bitcast_fusion.2
  238.8 0.2 copy.40
  239.0 87.6 %fusion.42 = f32[257,2,8,128]{0,1,3,2:T(2,128)S(1)} fusion(f32[2,1,7,7]{1,0,3,2:T(2,128)S(1)} %copy.40, bf16[257,1,14,134]{0,3,2,1:T(8,128)(2,1)} %bitcast.71), kind=kOutput, calls=%fused_computation.clone.1 | convolution fusion | flops 309485568 | bytes 3070000 | tf_op jit(solution)/shard_map/while/body/eval_jaxpr/conv_general_dilated | solution.py:42
  326.6 13.7 %multiply_reduce_fusion.4 = (f32[256,8,128]{0,2,1:T(8,128)S(1)}, f32[256,8,128]{0,2,1:T(8,128)S(1)}) fusion(f32[257,2,8,128]{0,1,3,2:T(2,128)S(1)} %fusion.42), kind=kLoop, calls=%fused_computation.3.clone.1 | loop fusion | flops 1835008 | bytes 6291456 | tf_op jit(solution)/shard_map/while/body/eval_jaxpr/mul | solution.py:49
  340.3 0.3 mul.70
  340.6 0.3 sub.13
  340.9 0.6 multiply_reduce_fusion.5
  341.6 0.7 dynamic-slice_bitcast_fusion.2
  342.3 0.2 copy.40
  342.5 87.6 %fusion.42 = f32[257,2,8,128]{0,1,3,2:T(2,128)S(1)} fusion(f32[2,1,7,7]{1,0,3,2:T(2,128)S(1)} %copy.40, bf16[257,1,14,134]{0,3,2,1:T(8,128)(2,1)} %bitcast.71), kind=kOutput, calls=%fused_computation.clone.1 | convolution fusion | flops 309485568 | bytes 3070000 | tf_op jit(solution)/shard_map/while/body/eval_jaxpr/conv_general_dilated | solution.py:42
  430.1 13.7 %multiply_reduce_fusion.4 = (f32[256,8,128]{0,2,1:T(8,128)S(1)}, f32[256,8,128]{0,2,1:T(8,128)S(1)}) fusion(f32[257,2,8,128]{0,1,3,2:T(2,128)S(1)} %fusion.42), kind=kLoop, calls=%fused_computation.3.clone.1 | loop fusion | flops 1835008 | bytes 6291456 | tf_op jit(solution)/shard_map/while/body/eval_jaxpr/mul | solution.py:49
  443.8 0.3 mul.70
  444.1 0.3 sub.13
  444.4 0.6 multiply_reduce_fusion.5
  445.2 0.9 convolution_bitcast_fusion
  446.2 0.0 all-reduce.2.cloned.1.call-update
  446.2 89.3 %all-reduce.2.cloned.1.call-done = f32[256,256]{1,0:T(8,128)} async-done(((f32[256,256]{1,0:T(8,128)}), f32[256,256]{1,0:T(8,128)}) %all-reduce.2.cloned.1.call-update) | async-done | bytes 262160 | tf_op jit(solution)/shard_map/psum | solution.py:59
  535.5 1.3 fusion.6
  536.8 0.2 fusion.25
  537.1 0.1 copy.28
  537.2 5.8 %cholesky.44 = f32[64,64]{1,0:T(8,128)S(1)} custom-call(f32[64,64]{1,0:T(8,128)S(1)} %fusion.18), custom_call_target="Cholesky" | custom-call | tf_op jit(solution)/shard_map/jit(cholesky)/cholesky | solution.py:28
  543.0 0.6 compare_reduce_fusion.1
  543.7 0.7 fusion.12
  544.3 4.9 custom-call.6
  549.2 0.3 convolution_bitcast_fusion.3
  549.5 1.3 fusion.4
  550.8 0.2 fusion.26
  551.1 0.1 copy.29
  551.1 5.8 %cholesky.55 = f32[64,64]{1,0:T(8,128)S(1)} custom-call(f32[64,64]{1,0:T(8,128)S(1)} %fusion.16), custom_call_target="Cholesky" | custom-call | tf_op jit(solution)/shard_map/jit(cholesky)/cholesky | solution.py:28
  557.0 0.6 compare_reduce_fusion
  557.7 0.7 fusion.13
  558.3 4.9 custom-call.7
  563.2 0.3 convolution_bitcast_fusion.2
  563.5 0.0 copy-start.1
  563.5 0.2 convolution_bitcast_fusion.1
  563.7 0.1 copy.30
  563.8 0.8 reshape.57
  (13 shorter events, 0.2 us)
Async XLA Ops:
  7.2 528.4 %copy-start = (f32[256,64]{0,1:T(8,128)S(1)}, f32[256,64]{0,1:T(8,128)}, u32[]{:S(2)}) copy-start(f32[256,64]{0,1:T(8,128)} %param.10) | copy-start | bytes 196612
  7.2 528.3 %all-reduce.2.cloned.1.call-start = ((), (), s32[]{:S(2)}) async-start(), calls=%async_computation | async-start | bytes 524288 | tf_op jit(solution)/shard_map/psum | solution.py:59
  8.8 8.2 %collective-permute-start = (bf16[257,3,128]{0,2,1:T(8,128)(2,1)S(1)}, bf16[257,3,128]{0,2,1:T(8,128)(2,1)S(1)}, u32[]{:S(2)}, u32[]{:S(2)}) collective-permute-start(bf16[257,3,128]{0,2,1:T(8,128)(2,1)S(1)} %get-tuple-element.39), channel_id=1, source_target_pairs={{0,4},{4,8},{8,12},{1,5},{5,9},{9,13},{2,6},{6,10},{10,14},{3,7},{... | collective-permute-start | bytes 592136 | tf_op jit(solution)/shard_map/ppermute | solution.py:20
  13.3 8.0 %collective-permute-start.1 = (bf16[257,3,128]{0,2,1:T(8,128)(2,1)S(1)}, bf16[257,3,128]{0,2,1:T(8,128)(2,1)S(1)}, u32[]{:S(2)}, u32[]{:S(2)}) collective-permute-start(bf16[257,3,128]{0,2,1:T(8,128)(2,1)S(1)} %get-tuple-element.40), channel_id=1, source_target_pairs={{4,0},{8,4},{12,8},{5,1},{9,5},{13,9},{6,2},{10,6},{14,10},{7,3},{... | collective-permute-start | bytes 592136 | tf_op jit(solution)/shard_map/ppermute | solution.py:21
  21.4 4.5 collective-permute-start.2
  24.6 4.8 collective-permute-start.3
  563.5 1.0 copy-start.1
Sparse Core Ops, SparseCore 0:
  446.3 89.1 all-reduce.1
where the time goes:
time: 572 us; the launch traced here: 571 us
  matrix products  355 us (62%)
  waiting for transfers between devices  98.9 us (17%)
  other arithmetic  83.2 us (15%)
  between operations  14.2 us (2%)
  starting transfers between devices  11 us (2%)
  local copies, waits for them, and re-layouts  8.54 us (1%)
    conv_general_dilated x4, matrix products, orient(): lax.conv_general_dilated(lifted, kernels, (1, 1), 'VALID', precision=lax....  350 us
    psum x1, waiting for transfers between devices, on_device(): gram = lax.psum(local_gram, ('row', 'col')) / npix_all  89.3 us
    mul x4, other arithmetic, orient(): prod_real * prod_real + prod_imag * prod_imag + 1.0  54.8 us
    another operation x6, other arithmetic, orthonormal(): factor = jnp.linalg.cholesky(inner)  13 us
  transfers between devices with their start and end apart: 5, of which 4 were waited for; matrix products, arithmetic and copies ran while one was open for 0% of the time, Pallas kernels for 0%

commit v1 on v0

--- a/solution.py
+++ b/solution.py
@@ -56,7 +56,7 @@
     npix_all = flat.shape[1] * devices_all
     basis_now = start_basis
     local_gram = jnp.dot(flat, flat.T, preferred_element_type=jnp.float32)
-    gram = lax.psum(local_gram, ("row", "col")) / npix_all
+    gram = lax.psum(lax.psum(local_gram, "col"), "row") / npix_all
     for sweep in range(SWEEPS):
         basis_now = orthonormal(jnp.dot(gram, basis_now, precision=lax.Precision.HIGHEST))
     projected = jnp.dot(basis_now.astype(jnp.bfloat16).T, flat, preferred_element_type=jnp.float32)

time: 572 us -> 552 us (0.965)
  waiting for transfers between devices: 98.9 us -> 77.2 us
    psum x1 -> x2, waiting for transfers between devices: 89.3 us -> 67.6 us  [on_device(): gram = lax.psum(lax.psum(local_gram, 'col'), 'row') / npix_all]
  transfers between devices with their start and end apart: 5 -> 6, of which waited for: 4 -> 5; matrix products, arithmetic and copies ran while one was open for 0% -> 0% of each run, Pallas kernels for 0% -> 0%
where the time goes in v1:
time: 552 us; the launch traced here: 550 us
  matrix products  355 us (64%)
  other arithmetic  83.2 us (15%)
  waiting for transfers between devices  77.2 us (14%)
  between operations  14.2 us (3%)
  starting transfers between devices  11.2 us (2%)
  local copies, waits for them, and re-layouts  8.53 us (2%)
    conv_general_dilated x4, matrix products, orient(): lax.conv_general_dilated(lifted, kernels, (1, 1), 'VALID', precision=lax....  350 us
    psum x2, waiting for transfers between devices, on_device(): gram = lax.psum(lax.psum(local_gram, 'col'), 'row') / npix_all  67.6 us
    mul x4, other arithmetic, orient(): prod_real * prod_real + prod_imag * prod_imag + 1.0  54.8 us
    another operation x6, other arithmetic, orthonormal(): factor = jnp.linalg.cholesky(inner)  13 us
    another operation x4, other arithmetic, orthonormal(): lax.linalg.triangular_solve(factor, stacked, left_side=False, lower=True,...  11.1 us
  transfers between devices with their start and end apart: 6, of which 5 were waited for; matrix products, arithmetic and copies ran while one was open for 0% of the time, Pallas kernels for 0%

profile of v1, /device:TPU:1, one launch (start us, length us, event | category | flops | bytes accessed | tf_op | source)
XLA Modules:
  0.0 549.7 jit_solution(4677316902731328907)
XLA Ops:
  7.2 0.0 all-reduce.3.cloned.1.call-start
  7.2 1.5 copy.25
  8.7 0.1 fusion.24
  8.8 4.5 collective-permute-start
  13.3 1.9 collective-permute-start.1
  15.2 1.7 collective-permute-done
  16.9 4.4 collective-permute-done.1
  21.4 3.2 collective-permute-start.2
  24.6 1.3 collective-permute-start.3
  25.9 3.4 collective-permute-done.3
  29.3 1.8 pad_maximum_fusion
  31.1 413.9 %while.10 = (s32[]{:T(128)}, bf16[4,256,2,32]{1,3,2,0:T(8,128)(2,1)S(1)}, bf16[257,14,134]{0,2,1:T(8,128)(2,1)}, f32[4,2,7,7]{3,1,2,0:T(2,128)}, s32[]{:T(128)}) while((s32[]{:T(128)}, bf16[4,256,2,32]{1,3,2,0:T(8,128)(2,1)S(1)}, bf16[257,14,134]{0,2,1:T(8,128)(2,1)}, f32[4,2,7,7]{3,1,2,0:T(2,128)}, s32[]{:T(128)}) %tuple.29), condition=%wide.region_2.3_spmd, body=%wide.region_0.2_spmd.sunk | while | flops 312647680 | bytes 15818389 | solution.py:53
  31.1 0.7 dynamic-slice_bitcast_fusion.2
  31.8 0.2 copy.40
  32.0 87.6 %fusion.42 = f32[257,2,8,128]{0,1,3,2:T(2,128)S(1)} fusion(f32[2,1,7,7]{1,0,3,2:T(2,128)S(1)} %copy.40, bf16[257,1,14,134]{0,3,2,1:T(8,128)(2,1)} %bitcast.71), kind=kOutput, calls=%fused_computation.clone.1 | convolution fusion | flops 309485568 | bytes 3070000 | tf_op jit(solution)/shard_map/while/body/eval_jaxpr/conv_general_dilated | solution.py:42
  119.6 13.7 %multiply_reduce_fusion.4 = (f32[256,8,128]{0,2,1:T(8,128)S(1)}, f32[256,8,128]{0,2,1:T(8,128)S(1)}) fusion(f32[257,2,8,128]{0,1,3,2:T(2,128)S(1)} %fusion.42), kind=kLoop, calls=%fused_computation.3.clone.1 | loop fusion | flops 1835008 | bytes 6291456 | tf_op jit(solution)/shard_map/while/body/eval_jaxpr/mul | solution.py:49
  133.3 0.3 mul.70
  133.6 0.3 sub.13
  134.0 0.6 multiply_reduce_fusion.5
  134.6 0.7 dynamic-slice_bitcast_fusion.2
  135.3 0.2 copy.40
  135.5 87.6 %fusion.42 = f32[257,2,8,128]{0,1,3,2:T(2,128)S(1)} fusion(f32[2,1,7,7]{1,0,3,2:T(2,128)S(1)} %copy.40, bf16[257,1,14,134]{0,3,2,1:T(8,128)(2,1)} %bitcast.71), kind=kOutput, calls=%fused_computation.clone.1 | convolution fusion | flops 309485568 | bytes 3070000 | tf_op jit(solution)/shard_map/while/body/eval_jaxpr/conv_general_dilated | solution.py:42
  223.1 13.7 %multiply_reduce_fusion.4 = (f32[256,8,128]{0,2,1:T(8,128)S(1)}, f32[256,8,128]{0,2,1:T(8,128)S(1)}) fusion(f32[257,2,8,128]{0,1,3,2:T(2,128)S(1)} %fusion.42), kind=kLoop, calls=%fused_computation.3.clone.1 | loop fusion | flops 1835008 | bytes 6291456 | tf_op jit(solution)/shard_map/while/body/eval_jaxpr/mul | solution.py:49
  236.8 0.3 mul.70
  237.1 0.3 sub.13
  237.4 0.6 multiply_reduce_fusion.5
  238.1 0.7 dynamic-slice_bitcast_fusion.2
  238.8 0.2 copy.40
  239.0 87.6 %fusion.42 = f32[257,2,8,128]{0,1,3,2:T(2,128)S(1)} fusion(f32[2,1,7,7]{1,0,3,2:T(2,128)S(1)} %copy.40, bf16[257,1,14,134]{0,3,2,1:T(8,128)(2,1)} %bitcast.71), kind=kOutput, calls=%fused_computation.clone.1 | convolution fusion | flops 309485568 | bytes 3070000 | tf_op jit(solution)/shard_map/while/body/eval_jaxpr/conv_general_dilated | solution.py:42
  326.6 13.7 %multiply_reduce_fusion.4 = (f32[256,8,128]{0,2,1:T(8,128)S(1)}, f32[256,8,128]{0,2,1:T(8,128)S(1)}) fusion(f32[257,2,8,128]{0,1,3,2:T(2,128)S(1)} %fusion.42), kind=kLoop, calls=%fused_computation.3.clone.1 | loop fusion | flops 1835008 | bytes 6291456 | tf_op jit(solution)/shard_map/while/body/eval_jaxpr/mul | solution.py:49
  340.3 0.3 mul.70
  340.6 0.3 sub.13
  340.9 0.6 multiply_reduce_fusion.5
  341.6 0.7 dynamic-slice_bitcast_fusion.2
  342.3 0.2 copy.40
  342.5 87.6 %fusion.42 = f32[257,2,8,128]{0,1,3,2:T(2,128)S(1)} fusion(f32[2,1,7,7]{1,0,3,2:T(2,128)S(1)} %copy.40, bf16[257,1,14,134]{0,3,2,1:T(8,128)(2,1)} %bitcast.71), kind=kOutput, calls=%fused_computation.clone.1 | convolution fusion | flops 309485568 | bytes 3070000 | tf_op jit(solution)/shard_map/while/body/eval_jaxpr/conv_general_dilated | solution.py:42
  430.1 13.7 %multiply_reduce_fusion.4 = (f32[256,8,128]{0,2,1:T(8,128)S(1)}, f32[256,8,128]{0,2,1:T(8,128)S(1)}) fusion(f32[257,2,8,128]{0,1,3,2:T(2,128)S(1)} %fusion.42), kind=kLoop, calls=%fused_computation.3.clone.1 | loop fusion | flops 1835008 | bytes 6291456 | tf_op jit(solution)/shard_map/while/body/eval_jaxpr/mul | solution.py:49
  443.8 0.3 mul.70
  444.1 0.3 sub.13
  444.4 0.6 multiply_reduce_fusion.5
  445.1 0.9 convolution_bitcast_fusion
  446.0 0.0 all-reduce.3.cloned.1.call-update
  446.0 0.2 all-reduce.5.cloned.1.call-start
  446.2 33.6 %all-reduce.3.cloned.1.call-done = f32[256,256]{1,0:T(8,128)} async-done(((f32[256,256]{1,0:T(8,128)}), f32[256,256]{1,0:T(8,128)}) %all-reduce.3.cloned.1.call-update) | async-done | bytes 262160 | tf_op jit(solution)/shard_map/psum | solution.py:59
  479.8 34.0 %all-reduce.5.cloned.1.call-done = f32[256,256]{1,0:T(8,128)} async-done(((f32[256,256]{1,0:T(8,128)}), f32[256,256]{1,0:T(8,128)}) %all-reduce.5.cloned.1.call-update) | async-done | bytes 262160 | tf_op jit(solution)/shard_map/psum | solution.py:59
  513.9 1.3 fusion.6
  515.2 0.2 fusion.25
  515.4 0.1 copy.28
  515.5 5.8 %cholesky.44 = f32[64,64]{1,0:T(8,128)S(1)} custom-call(f32[64,64]{1,0:T(8,128)S(1)} %fusion.18), custom_call_target="Cholesky" | custom-call | tf_op jit(solution)/shard_map/jit(cholesky)/cholesky | solution.py:28
  521.4 0.6 compare_reduce_fusion.1
  522.0 0.7 fusion.12
  522.7 4.9 custom-call.6
  527.6 0.3 convolution_bitcast_fusion.3
  527.8 1.3 fusion.4
  529.2 0.2 fusion.26
  529.4 0.1 copy.29
  529.5 5.8 %cholesky.55 = f32[64,64]{1,0:T(8,128)S(1)} custom-call(f32[64,64]{1,0:T(8,128)S(1)} %fusion.16), custom_call_target="Cholesky" | custom-call | tf_op jit(solution)/shard_map/jit(cholesky)/cholesky | solution.py:28
  535.4 0.6 compare_reduce_fusion
  536.0 0.7 fusion.13
  536.7 4.9 custom-call.7
  541.6 0.3 convolution_bitcast_fusion.2
  541.8 0.2 convolution_bitcast_fusion.1
  542.0 0.1 copy.30
  542.1 0.8 reshape.57
  (16 shorter events, 0.2 us)
Async XLA Ops:
  7.2 506.7 %copy-start = (f32[256,64]{0,1:T(8,128)S(1)}, f32[256,64]{0,1:T(8,128)}, u32[]{:S(2)}) copy-start(f32[256,64]{0,1:T(8,128)} %param.10) | copy-start | bytes 196612
  7.2 472.6 %all-reduce.3.cloned.1.call-start = ((), (), s32[]{:S(2)}) async-start(), calls=%async_computation | async-start | bytes 524288 | tf_op jit(solution)/shard_map/psum | solution.py:59
  8.8 8.2 %collective-permute-start = (bf16[257,3,128]{0,2,1:T(8,128)(2,1)S(1)}, bf16[257,3,128]{0,2,1:T(8,128)(2,1)S(1)}, u32[]{:S(2)}, u32[]{:S(2)}) collective-permute-start(bf16[257,3,128]{0,2,1:T(8,128)(2,1)S(1)} %get-tuple-element.39), channel_id=1, source_target_pairs={{0,4},{4,8},{8,12},{1,5},{5,9},{9,13},{2,6},{6,10},{10,14},{3,7},{... | collective-permute-start | bytes 592136 | tf_op jit(solution)/shard_map/ppermute | solution.py:20
  13.3 8.0 %collective-permute-start.1 = (bf16[257,3,128]{0,2,1:T(8,128)(2,1)S(1)}, bf16[257,3,128]{0,2,1:T(8,128)(2,1)S(1)}, u32[]{:S(2)}, u32[]{:S(2)}) collective-permute-start(bf16[257,3,128]{0,2,1:T(8,128)(2,1)S(1)} %get-tuple-element.40), channel_id=1, source_target_pairs={{4,0},{8,4},{12,8},{5,1},{9,5},{13,9},{6,2},{10,6},{14,10},{7,3},{... | collective-permute-start | bytes 592136 | tf_op jit(solution)/shard_map/ppermute | solution.py:21
  21.4 4.5 collective-permute-start.2
  24.6 4.8 collective-permute-start.3
  446.0 67.8 %all-reduce.5.cloned.1.call-start = ((), (), s32[]{:S(2)}) async-start(), calls=%async_computation.1 | async-start | bytes 524288 | tf_op jit(solution)/shard_map/psum | solution.py:59
  541.8 1.0 copy-start.1
Sparse Core Ops, SparseCore 0:
  446.1 33.6 all-reduce.2
  482.2 31.5 all-reduce.4
